TPU v7x, 128 devices: a whole 4x4x4 slice. The times are simulated.
128 devices in a mesh: doc: 16 (over y, z), own: 8 (over x, core).
Axes of the slice: x: 4, y: 4, z: 4, core: 2. Of those that a mesh axis runs over, the one named last changes fastest.
Arguments:
- embeddings: bfloat16 [65536, 768], P(('doc', 'own')), may hold values from -6 to 6
- cluster_ids: int32 [65536], P(('doc', 'own')), may hold values from 0 to 50175, as said below
- keep_flags: int32 [65536], P(('doc', 'own')), may hold values 0 or 1
Outputs:
- centroids: bfloat16 [50176, 768], P(('doc', 'own'))
- scores: float32 [65536], P(('doc', 'own'))
Inputs may be any that keep to these rules, and one draw needn't show every extreme that they name: `cluster_ids`: cluster c is held by device c // 392 of the rows' order. Among the rows of one device, at most 8 name clusters held by any one device, and exactly 8 do for one device.
All inputs are finite; a program needn't handle non-finite values. No bound on the sum of `keep_flags` on one device may be relied on, other than what follows from the above.
Results may differ from a plain program's by a relative error of at most 0.0015.
Values may be sent and summed in bfloat16 or wider, within the bound.
No kernel may reach another device: no remote copies, remote signals or barrier semaphores. Data moves between devices by JAX's collectives and lax.ppermute only.
A program may use at most 64 MiB of HBM per device.

v0:
```python
import math
import jax
import jax.numpy as jnp
from jax import lax
from jax.sharding import PartitionSpec as P

CLUSTER_DEV = 392


def unit_rows(sums, width):
    inv_scale = lax.rsqrt(jnp.mean(sums * sums, axis=1, keepdims=True) + 1e-06) / math.sqrt(width)
    return (sums * inv_scale).astype(jnp.bfloat16)


def pack_rows(embeddings, slot_code, slot, slots_total):
    width = embeddings.shape[1]
    outgoing = jnp.zeros((slots_total, width), jnp.bfloat16).at[slot].set(embeddings)
    codes_out = jnp.full((slots_total,), -1, jnp.int32).at[slot].set(slot_code)
    return (outgoing, codes_out)


def body(embeddings, cluster_ids, keep_flags):
    row_count = embeddings.shape[0]
    width = embeddings.shape[1]
    grid_size = lax.axis_size(("doc", "own"))
    doc_count = lax.axis_size("doc")
    own_count = lax.axis_size("own")
    capacity = 2 * row_count // grid_size
    slots_total = grid_size * capacity
    per_device = CLUSTER_DEV
    target = cluster_ids // per_device
    local_id = cluster_ids % per_device
    hits = (target[:, None] == jnp.arange(grid_size, dtype=jnp.int32)[None, :]).astype(jnp.int32)
    position = jnp.sum(jnp.cumsum(hits, axis=0) * hits, axis=1) - 1
    slot_code = local_id + per_device * keep_flags
    row_scale = lax.rsqrt(
        jnp.mean(jnp.square(embeddings.astype(jnp.float32)), axis=1) + 1e-06
    ) / math.sqrt(width)
    slot = (target % own_count * doc_count + target // own_count) * capacity + position
    outgoing, codes_out = pack_rows(embeddings, slot_code, slot, slots_total)
    arrived, codes_in = (
        lax.all_to_all(outgoing, "own", split_axis=0, concat_axis=0, tiled=True),
        lax.all_to_all(codes_out, "own", split_axis=0, concat_axis=0, tiled=True),
    )
    slot_doc = jnp.arange(slots_total, dtype=jnp.int32) // capacity % doc_count
    valid = codes_in >= 0
    owner_index = jnp.where(valid, slot_doc * per_device + codes_in % per_device, -1)
    weight = jnp.where(valid, codes_in // per_device, 0)
    labels = jnp.arange(per_device * lax.axis_size("doc"), dtype=jnp.int32)
    table = ((labels[:, None] == owner_index[None, :]) * weight[None, :]).astype(jnp.bfloat16)
    sums = lax.psum_scatter(
        jnp.dot(table, arrived, preferred_element_type=jnp.float32),
        "doc",
        scatter_dimension=0,
        tiled=True,
    )
    centroids = unit_rows(sums, width)
    piece = lax.all_gather(centroids, "doc", axis=0, tiled=True)
    similar = jnp.dot(arrived, piece.T, preferred_element_type=jnp.float32)
    column = owner_index - jnp.int32(0)
    chosen = column[:, None] == jnp.arange(piece.shape[0], dtype=jnp.int32)[None, :]
    products = jnp.sum(jnp.where(chosen, similar, 0.0), axis=1)
    returned = lax.all_to_all(products, "own", split_axis=0, concat_axis=0, tiled=True)
    scores = returned[slot] * row_scale
    return (centroids, scores)


def solution(mesh):
    in_specs = (P(("doc", "own"), None), P(("doc", "own")), P(("doc", "own")))
    out_specs = (P(("doc", "own"), None), P(("doc", "own")))
    return jax.shard_map(body, mesh=mesh, in_specs=in_specs, out_specs=out_specs, check_vma=False)
```

profile of v0, /device:TPU:1, one launch (start us, length us, event | category | flops | bytes accessed | tf_op | source)
XLA Modules:
  0.0 299.3 jit_solution(1905121783948206056)
XLA Ops:
  7.2 0.0 copy-start.1
  7.2 0.8 fusion.25
  8.0 0.1 copy.7
  8.1 0.2 fusion.7
  8.4 0.2 fusion.6
  8.6 3.0 %scatter_custom_fusion = s32[1024]{0:T(1024)} fusion(s32[512]{0:T(512)S(1)} %compare_select_fusion, s32[512]{0:T(512)S(1)} %get-tuple-element.4, s32[]{:T(128)} %constant.95.clone.1), kind=kCustom, calls=%fused_computation.66 | custom fusion | bytes 4100 | tf_op jit(solution)/shard_map/scatter | solution.py:18
  11.7 5.8 %all-to-all-start = ((s32[8,128,1]{1,2,0:T(1,128)}), s32[8,128,1]{1,2,0:T(1,128)S(1)}, u32[]{:S(2)}, u32[]{:S(2)}) async-start(s32[8,128,1]{1,2,0:T(1,128)} %bitcast.5), calls=%async_computation | async-start | bytes 8192 | tf_op jit(solution)/shard_map/all_to_all | solution.py:43
  17.5 0.0 copy-done.1
  17.5 3.8 %scatter_custom_fusion.1 = bf16[1024,768]{1,0:T(8,128)(2,1)} fusion(s32[512]{0:T(512)S(1)} %compare_select_fusion, bf16[512,768]{1,0:T(8,128)(2,1)S(1)} %copy-done.1, bf16[]{:T(256)} %constant.105.clone.1), kind=kCustom, calls=%fused_computation.14 | custom fusion | bytes 1572866 | tf_op jit(solution)/shard_map/scatter | solution.py:17
  21.3 0.7 all-to-all-done
  22.0 4.2 %all-to-all-start.1 = ((bf16[8,128,768]{2,1,0:T(8,128)(2,1)}), bf16[8,128,768]{2,1,0:T(8,128)(2,1)S(1)}, u32[]{:S(2)}, u32[]{:S(2)}) async-start(bf16[8,128,768]{2,1,0:T(8,128)(2,1)} %bitcast.14), calls=%async_computation.1 | async-start | bytes 3145728 | tf_op jit(solution)/shard_map/all_to_all | solution.py:42
  26.1 0.0 reduce-scatter.4.cloned.1.call-start
  26.2 20.7 %all-to-all-done.1 = bf16[8,128,768]{2,1,0:T(8,128)(2,1)S(1)} async-done(((bf16[8,128,768]{2,1,0:T(8,128)(2,1)}), bf16[8,128,768]{2,1,0:T(8,128)(2,1)S(1)}, u32[]{:S(2)}, u32[]{:S(2)}) %all-to-all-start.1) | async-done | bytes 1572896 | tf_op jit(solution)/shard_map/all_to_all | solution.py:42
  46.9 13.4 %fusion = f32[6272,768]{1,0:T(8,128)} fusion(bf16[1024,768]{1,0:T(8,128)(2,1)S(1)} %bitcast.53, s32[1024]{0:T(1024)S(1)} %get-tuple-element.3, s32[1024]{0:T(1024)S(1)} %get-tuple-element.2), kind=kOutput, calls=%fused_computation.7 | convolution fusion | flops 9884270592 | bytes 20848640 | tf_op jit(solution)/shard_map/dot_general | solution.py:52
  60.2 0.0 reduce-scatter.4.cloned.1.call-update
  60.2 0.0 all-gather.2.cloned.1.call-start
  60.3 124.5 %reduce-scatter.4.cloned.1.call-done = f32[392,768]{1,0:T(8,128)} async-done(((f32[6272,768]{1,0:T(8,128)}), f32[392,768]{1,0:T(8,128)}) %reduce-scatter.4.cloned.1.call-update) | async-done | bytes 1204240
  184.8 0.0 copy-start
  184.8 1.5 multiply_reduce_fusion.1
  186.4 0.1 copy-done
  186.5 0.9 multiply_convert_fusion
  187.4 0.0 all-gather.2.cloned.1.call-update
  187.5 0.2 multiply_reduce_fusion
  187.7 76.4 %all-gather.2.cloned.1.call-done = bf16[6272,768]{1,0:T(8,128)(2,1)} async-done(((bf16[392,768]{1,0:T(8,128)(2,1)}), bf16[6272,768]{1,0:T(8,128)(2,1)}) %all-gather.2.cloned.1.call-update) | async-done | bytes 9633808 | tf_op jit(solution)/shard_map/all_gather | solution.py:58
  264.1 16.0 %select_reduce_fusion = f32[1024]{0:T(1024)} fusion(bf16[1024,768]{1,0:T(8,128)(2,1)S(1)} %bitcast.54, bf16[6272,768]{1,0:T(8,128)(2,1)} %all-gather.2.cloned.1.call-done, s32[1024]{0:T(1024)S(1)} %get-tuple-element.2), kind=kOutput, calls=%fused_computation.3 | convolution fusion | flops 9884269568 | bytes 11214848 | tf_op jit(solution)/shard_map/dot_general | solution.py:59
  280.1 4.9 %all-to-all-start.2 = ((f32[8,128,1]{1,2,0:T(1,128)}), f32[8,128,1]{1,2,0:T(1,128)S(1)}, u32[]{:S(2)}, u32[]{:S(2)}) async-start(f32[8,128,1]{1,2,0:T(1,128)} %bitcast.17), calls=%async_computation.2 | async-start | bytes 8192 | tf_op jit(solution)/shard_map/all_to_all | solution.py:63
  285.0 4.6 %all-to-all-done.2 = f32[8,128,1]{1,2,0:T(1,128)S(1)} async-done(((f32[8,128,1]{1,2,0:T(1,128)}), f32[8,128,1]{1,2,0:T(1,128)S(1)}, u32[]{:S(2)}, u32[]{:S(2)}) %all-to-all-start.2) | async-done | bytes 4128 | tf_op jit(solution)/shard_map/all_to_all | solution.py:63
  289.6 2.3 gather_fusion
  291.8 0.6 multiply_multiply_fusion
  (10 shorter events, 0.1 us)
Async XLA Ops:
  7.2 10.3 %copy-start.1 = (bf16[512,768]{1,0:T(8,128)(2,1)S(1)}, bf16[512,768]{1,0:T(8,128)(2,1)}, u32[]{:S(2)}) copy-start(bf16[512,768]{1,0:T(8,128)(2,1)} %param.3) | copy-start | bytes 2359300
  11.7 10.3 %all-to-all-start = ((s32[8,128,1]{1,2,0:T(1,128)}), s32[8,128,1]{1,2,0:T(1,128)S(1)}, u32[]{:S(2)}, u32[]{:S(2)}) async-start(s32[8,128,1]{1,2,0:T(1,128)} %bitcast.5), calls=%async_computation | async-start | bytes 8192 | tf_op jit(solution)/shard_map/all_to_all | solution.py:43
  22.0 24.9 %all-to-all-start.1 = ((bf16[8,128,768]{2,1,0:T(8,128)(2,1)}), bf16[8,128,768]{2,1,0:T(8,128)(2,1)S(1)}, u32[]{:S(2)}, u32[]{:S(2)}) async-start(bf16[8,128,768]{2,1,0:T(8,128)(2,1)} %bitcast.14), calls=%async_computation.1 | async-start | bytes 3145728 | tf_op jit(solution)/shard_map/all_to_all | solution.py:42
  26.1 158.7 %reduce-scatter.4.cloned.1.call-start = ((), (), s32[]{:S(2)}) async-start(), calls=%async_computation.5 | async-start | bytes 20471808
  60.2 203.9 %all-gather.2.cloned.1.call-start = ((), (), s32[]{:S(2)}) async-start(), calls=%async_computation.4 | async-start | bytes 10235904 | tf_op jit(solution)/shard_map/all_gather | solution.py:58
  184.8 1.6 copy-start
  280.1 9.5 %all-to-all-start.2 = ((f32[8,128,1]{1,2,0:T(1,128)}), f32[8,128,1]{1,2,0:T(1,128)S(1)}, u32[]{:S(2)}, u32[]{:S(2)}) async-start(f32[8,128,1]{1,2,0:T(1,128)} %bitcast.17), calls=%async_computation.2 | async-start | bytes 8192 | tf_op jit(solution)/shard_map/all_to_all | solution.py:63
Sparse Core Ops, SparseCore 0:
  60.4 124.4 reduce-scatter.3
  187.8 76.2 all-gather.1
where the time goes:
time: 300 us; the launch traced here: 299 us
  waiting for transfers between devices  227 us (76%)
  matrix products  29.3 us (10%)
  starting transfers between devices  14.9 us (5%)
  between operations  14.1 us (5%)
  local copies, waits for them, and re-layouts  9.33 us (3%)
  other arithmetic  4.63 us (2%)
    unnamed x3, waiting for transfers between devices  125 us
    all_gather x1, waiting for transfers between devices, body(): piece = lax.all_gather(centroids, 'doc', axis=0, tiled=True)  76.4 us
    all_to_all x1, waiting for transfers between devices, body(): lax.all_to_all(outgoing, 'own', split_axis=0, concat_axis=0, tiled=True)  20.7 us
    dot_general x1, matrix products, body(): similar = jnp.dot(arrived, piece.T, preferred_element_type=jnp.float32)  16 us
    dot_general x1, matrix products, body(): jnp.dot(table, arrived, preferred_element_type=jnp.float32)  13.4 us
  transfers between devices with their start and end apart: 5, of which 5 were waited for; matrix products, arithmetic and copies ran while one was open for 1% of the time, Pallas kernels for 0%

commit v1 on v0

--- a/solution.py
+++ b/solution.py
@@ -5,6 +5,18 @@
 from jax.sharding import PartitionSpec as P
 
 CLUSTER_DEV = 392
+
+
+def wires_update(axis_tag, matrix):
+    wide_n = lax.axis_size(axis_tag)
+    frame_out = sorted(((pp, (pp + 1) % wide_n) for pp in range(wide_n)))
+    p_next = matrix
+    tray = [p_next]
+    for kk in range(1, wide_n):
+        p_next = lax.ppermute(p_next, axis_tag, frame_out)
+        tray.insert(0, p_next)
+    row_out = jnp.concatenate(tray, 0)
+    return jnp.roll(row_out, (lax.axis_index(axis_tag) + 1) * matrix.shape[0], 0)
 
 
 def unit_rows(sums, width):
@@ -55,7 +67,7 @@
         tiled=True,
     )
     centroids = unit_rows(sums, width)
-    piece = lax.all_gather(centroids, "doc", axis=0, tiled=True)
+    piece = wires_update("doc", centroids)
     similar = jnp.dot(arrived, piece.T, preferred_element_type=jnp.float32)
     column = owner_index - jnp.int32(0)
     chosen = column[:, None] == jnp.arange(piece.shape[0], dtype=jnp.int32)[None, :]

time: 300 us -> 526 us (1.75)
  waiting for transfers between devices: 227 us -> 378 us
  local copies, waits for them, and re-layouts: 9.33 us -> 59.5 us
  starting transfers between devices: 14.9 us -> 32.4 us
    ppermute x0 -> x15, waiting for transfers between devices: none -> 228 us  [wires_update(): p_next = lax.ppermute(p_next, axis_tag, frame_out)]
    all_gather x1 -> x0, waiting for transfers between devices: 76.4 us -> none  [body(): piece = lax.all_gather(centroids, 'doc', axis=0, tiled=True)]
    unnamed x5 -> x79, local copies, waits for them, and re-layouts: 0.1 us -> 49.7 us
    all_to_all x1, starting transfers between devices: 4.92 us -> 20.6 us  [body(): lax.all_to_all(products, 'own', split_axis=0, concat_axis=0, tiled=True)]
    unnamed x3 -> x2, waiting for transfers between devices: 125 us -> 124 us
  transfers between devices with their start and end apart: 5 -> 19, of which waited for: 5 -> 19; matrix products, arithmetic and copies ran while one was open for 1% -> 1% of each run, Pallas kernels for 0% -> 0%
where the time goes in v1:
time: 526 us; the launch traced here: 525 us
  waiting for transfers between devices  378 us (72%)
  local copies, waits for them, and re-layouts  59.5 us (11%)
  matrix products  33 us (6%)
  starting transfers between devices  32.4 us (6%)
  between operations  14.2 us (3%)
  other arithmetic  8.21 us (2%)
    ppermute x15, waiting for transfers between devices, wires_update(): p_next = lax.ppermute(p_next, axis_tag, frame_out)  228 us
    unnamed x2, waiting for transfers between devices  124 us
    unnamed x79, local copies, waits for them, and re-layouts  49.7 us
    all_to_all x1, waiting for transfers between devices, body(): lax.all_to_all(outgoing, 'own', split_axis=0, concat_axis=0, tiled=True)  20.7 us
    all_to_all x1, starting transfers between devices, body(): lax.all_to_all(products, 'own', split_axis=0, concat_axis=0, tiled=True)  20.6 us
    dot_general x1, matrix products, body(): similar = jnp.dot(arrived, piece.T, preferred_element_type=jnp.float32)  19.7 us
    dot_general x1, matrix products, body(): jnp.dot(table, arrived, preferred_element_type=jnp.float32)  13.3 us
  transfers between devices with their start and end apart: 19, of which 19 were waited for; matrix products, arithmetic and copies ran while one was open for 1% of the time, Pallas kernels for 0%

profile of v1, /device:TPU:1, one launch (start us, length us, event | category | flops | bytes accessed | tf_op | source)
XLA Modules:
  0.0 525.1 jit_solution(6474274193660067909)
XLA Ops:
  8.6 3.0 scatter_custom_fusion
  11.6 5.8 %all-to-all-start = ((s32[8,128,1]{1,2,0:T(1,128)}), s32[8,128,1]{1,2,0:T(1,128)S(1)}, u32[]{:S(2)}, u32[]{:S(2)}) async-start(s32[8,128,1]{1,2,0:T(1,128)} %bitcast.5), calls=%async_computation | async-start | bytes 8192 | tf_op jit(solution)/shard_map/all_to_all | solution.py:55
  17.4 4.4 scatter_custom_fusion.1
  21.9 4.7 all-to-all-start.1
  26.6 20.7 %all-to-all-done.1 = bf16[8,128,768]{2,1,0:T(8,128)(2,1)S(1)} async-done(((bf16[8,128,768]{2,1,0:T(8,128)(2,1)}), bf16[8,128,768]{2,1,0:T(8,128)(2,1)S(1)}, u32[]{:S(2)}, u32[]{:S(2)}) %all-to-all-start.1) | async-done | bytes 1572896 | tf_op jit(solution)/shard_map/all_to_all | solution.py:54
  47.3 13.3 %fusion = f32[6272,768]{1,0:T(8,128)} fusion(bf16[1024,768]{1,0:T(8,128)(2,1)S(1)} %bitcast.52, s32[1024]{0:T(1024)S(1)} %get-tuple-element.3, s32[1024]{0:T(1024)S(1)} %get-tuple-element.2), kind=kOutput, calls=%fused_computation.7 | convolution fusion | flops 9884270592 | bytes 20848640 | tf_op jit(solution)/shard_map/dot_general | solution.py:64
  60.6 124.5 %reduce-scatter.4.cloned.1.call-done = f32[392,768]{1,0:T(8,128)} async-done(((f32[6272,768]{1,0:T(8,128)}), f32[392,768]{1,0:T(8,128)}) %reduce-scatter.4.cloned.1.call-update) | async-done | bytes 1204240
  185.1 1.5 multiply_reduce_fusion.1
  186.7 1.4 multiply_convert_fusion
  188.1 1.2 collective-permute-start
  189.4 16.5 %collective-permute-done = bf16[392,768]{1,0:T(8,128)(2,1)S(1)} collective-permute-done((bf16[392,768]{1,0:T(8,128)(2,1)S(1)}, bf16[392,768]{1,0:T(8,128)(2,1)S(1)}, u32[]{:S(2)}, u32[]{:S(2)}) %collective-permute-start) | collective-permute-done | bytes 602144 | tf_op jit(solution)/shard_map/ppermute | solution.py:16
  205.9 16.8 %collective-permute-done.1 = bf16[392,768]{1,0:T(8,128)(2,1)S(1)} collective-permute-done((bf16[392,768]{1,0:T(8,128)(2,1)S(1)}, bf16[392,768]{1,0:T(8,128)(2,1)S(1)}, u32[]{:S(2)}, u32[]{:S(2)}) %collective-permute-start.1) | collective-permute-done | bytes 602144 | tf_op jit(solution)/shard_map/ppermute | solution.py:16
  222.7 15.9 %collective-permute-done.2 = bf16[392,768]{1,0:T(8,128)(2,1)S(1)} collective-permute-done((bf16[392,768]{1,0:T(8,128)(2,1)S(1)}, bf16[392,768]{1,0:T(8,128)(2,1)S(1)}, u32[]{:S(2)}, u32[]{:S(2)}) %collective-permute-start.2) | collective-permute-done | bytes 602144 | tf_op jit(solution)/shard_map/ppermute | solution.py:16
  238.6 14.9 %collective-permute-done.3 = bf16[392,768]{1,0:T(8,128)(2,1)S(1)} collective-permute-done((bf16[392,768]{1,0:T(8,128)(2,1)S(1)}, bf16[392,768]{1,0:T(8,128)(2,1)S(1)}, u32[]{:S(2)}, u32[]{:S(2)}) %collective-permute-start.3) | collective-permute-done | bytes 602144 | tf_op jit(solution)/shard_map/ppermute | solution.py:16
  254.3 14.0 %collective-permute-done.4 = bf16[392,768]{1,0:T(8,128)(2,1)S(1)} collective-permute-done((bf16[392,768]{1,0:T(8,128)(2,1)S(1)}, bf16[392,768]{1,0:T(8,128)(2,1)S(1)}, u32[]{:S(2)}, u32[]{:S(2)}) %collective-permute-start.4) | collective-permute-done | bytes 602144 | tf_op jit(solution)/shard_map/ppermute | solution.py:16
  269.2 13.1 %collective-permute-done.5 = bf16[392,768]{1,0:T(8,128)(2,1)S(1)} collective-permute-done((bf16[392,768]{1,0:T(8,128)(2,1)S(1)}, bf16[392,768]{1,0:T(8,128)(2,1)S(1)}, u32[]{:S(2)}, u32[]{:S(2)}) %collective-permute-start.5) | collective-permute-done | bytes 602144 | tf_op jit(solution)/shard_map/ppermute | solution.py:16
  283.1 12.2 %collective-permute-done.6 = bf16[392,768]{1,0:T(8,128)(2,1)S(1)} collective-permute-done((bf16[392,768]{1,0:T(8,128)(2,1)S(1)}, bf16[392,768]{1,0:T(8,128)(2,1)S(1)}, u32[]{:S(2)}, u32[]{:S(2)}) %collective-permute-start.6) | collective-permute-done | bytes 602144 | tf_op jit(solution)/shard_map/ppermute | solution.py:16
  296.1 12.3 %collective-permute-done.7 = bf16[392,768]{1,0:T(8,128)(2,1)S(1)} collective-permute-done((bf16[392,768]{1,0:T(8,128)(2,1)S(1)}, bf16[392,768]{1,0:T(8,128)(2,1)S(1)}, u32[]{:S(2)}, u32[]{:S(2)}) %collective-permute-start.7) | collective-permute-done | bytes 602144 | tf_op jit(solution)/shard_map/ppermute | solution.py:16
  308.4 0.9 copy-done.9
  309.3 13.3 %collective-permute-done.8 = bf16[392,768]{1,0:T(8,128)(2,1)S(1)} collective-permute-done((bf16[392,768]{1,0:T(8,128)(2,1)S(1)}, bf16[392,768]{1,0:T(8,128)(2,1)S(1)}, u32[]{:S(2)}, u32[]{:S(2)}) %collective-permute-start.8) | collective-permute-done | bytes 602144 | tf_op jit(solution)/shard_map/ppermute | solution.py:16
  322.7 0.9 copy-done.11
  323.6 14.4 %collective-permute-done.9 = bf16[392,768]{1,0:T(8,128)(2,1)S(1)} collective-permute-done((bf16[392,768]{1,0:T(8,128)(2,1)S(1)}, bf16[392,768]{1,0:T(8,128)(2,1)S(1)}, u32[]{:S(2)}, u32[]{:S(2)}) %collective-permute-start.9) | collective-permute-done | bytes 602144 | tf_op jit(solution)/shard_map/ppermute | solution.py:16
  338.8 15.6 %collective-permute-done.10 = bf16[392,768]{1,0:T(8,128)(2,1)S(1)} collective-permute-done((bf16[392,768]{1,0:T(8,128)(2,1)S(1)}, bf16[392,768]{1,0:T(8,128)(2,1)S(1)}, u32[]{:S(2)}, u32[]{:S(2)}) %collective-permute-start.10) | collective-permute-done | bytes 602144 | tf_op jit(solution)/shard_map/ppermute | solution.py:16
  355.1 16.6 %collective-permute-done.11 = bf16[392,768]{1,0:T(8,128)(2,1)S(1)} collective-permute-done((bf16[392,768]{1,0:T(8,128)(2,1)S(1)}, bf16[392,768]{1,0:T(8,128)(2,1)S(1)}, u32[]{:S(2)}, u32[]{:S(2)}) %collective-permute-start.11) | collective-permute-done | bytes 602144 | tf_op jit(solution)/shard_map/ppermute | solution.py:16
  372.6 17.7 %collective-permute-done.12 = bf16[392,768]{1,0:T(8,128)(2,1)S(1)} collective-permute-done((bf16[392,768]{1,0:T(8,128)(2,1)S(1)}, bf16[392,768]{1,0:T(8,128)(2,1)S(1)}, u32[]{:S(2)}, u32[]{:S(2)}) %collective-permute-start.12) | collective-permute-done | bytes 602144 | tf_op jit(solution)/shard_map/ppermute | solution.py:16
  391.2 18.7 %collective-permute-done.13 = bf16[392,768]{1,0:T(8,128)(2,1)} collective-permute-done((bf16[392,768]{1,0:T(8,128)(2,1)S(1)}, bf16[392,768]{1,0:T(8,128)(2,1)}, u32[]{:S(2)}, u32[]{:S(2)}) %collective-permute-start.13) | collective-permute-done | bytes 602144 | tf_op jit(solution)/shard_map/ppermute | solution.py:16
  410.0 1.5 multiply_reduce_fusion
  411.5 15.9 %collective-permute-done.14 = bf16[392,768]{1,0:T(8,128)(2,1)} collective-permute-done((bf16[392,768]{1,0:T(8,128)(2,1)}, bf16[392,768]{1,0:T(8,128)(2,1)}, u32[]{:S(2)}, u32[]{:S(2)}) %collective-permute-start.14) | collective-permute-done | bytes 602144 | tf_op jit(solution)/shard_map/ppermute | solution.py:16
  427.3 1.9 constant_dynamic-update-slice_fusion.31
  429.3 2.1 constant_dynamic-update-slice_fusion.30
  431.3 1.9 constant_dynamic-update-slice_fusion.29
  433.3 1.9 constant_dynamic-update-slice_fusion.28
  435.2 1.9 constant_dynamic-update-slice_fusion.27
  437.1 1.9 constant_dynamic-update-slice_fusion.26
  439.1 1.9 constant_dynamic-update-slice_fusion.25
  441.0 1.9 constant_dynamic-update-slice_fusion.24
  442.9 1.9 constant_dynamic-update-slice_fusion.23
  444.9 1.9 constant_dynamic-update-slice_fusion.22
  446.8 1.9 constant_dynamic-update-slice_fusion.21
  448.7 1.9 constant_dynamic-update-slice_fusion.20
  450.7 0.9 constant_dynamic-update-slice_fusion.19
  451.5 0.9 constant_dynamic-update-slice_fusion.18
  452.4 0.9 constant_dynamic-update-slice_fusion.17
  453.4 0.9 constant_dynamic-update-slice_fusion.16
  454.3 1.9 constant_dynamic-update-slice_fusion.15
  456.2 1.9 constant_dynamic-update-slice_fusion.14
  458.2 0.9 constant_dynamic-update-slice_fusion.13
  459.0 0.9 constant_dynamic-update-slice_fusion.12
  459.9 0.9 constant_dynamic-update-slice_fusion.11
  460.8 0.9 constant_dynamic-update-slice_fusion.10
  461.7 0.9 constant_dynamic-update-slice_fusion.9
  462.6 0.9 constant_dynamic-update-slice_fusion.8
  463.4 0.9 constant_dynamic-update-slice_fusion.7
  464.3 0.9 constant_dynamic-update-slice_fusion.6
  465.2 0.9 constant_dynamic-update-slice_fusion.5
  466.1 0.9 constant_dynamic-update-slice_fusion.4
  467.0 0.9 constant_dynamic-update-slice_fusion.3
  467.8 0.9 constant_dynamic-update-slice_fusion.2
  468.7 0.9 constant_dynamic-update-slice_fusion.1
  469.6 1.0 constant_dynamic-update-slice_fusion
  470.5 19.7 %select_reduce_fusion = f32[1024]{0:T(1024)} fusion(bf16[1024,768]{1,0:T(8,128)(2,1)S(1)} %bitcast.53, s32[1024]{0:T(1024)S(1)} %get-tuple-element.2, bf16[12544,768]{1,0:T(8,128)(2,1)} %constant_dynamic-update-slice_fusion, s32[]{:T(128)S(6)} %select_n.117), kind=kOutput, calls=%fused_computation.3 | convolution fusion | flops 9884269568 | bytes 11214852 | tf_op jit(solution)/shard_map/dot_general | solution.py:71
  490.2 20.6 %all-to-all-start.2 = ((f32[8,128,1]{1,2,0:T(1,128)}), f32[8,128,1]{1,2,0:T(1,128)S(1)}, u32[]{:S(2)}, u32[]{:S(2)}) async-start(f32[8,128,1]{1,2,0:T(1,128)} %bitcast.17), calls=%async_computation.2 | async-start | bytes 8192 | tf_op jit(solution)/shard_map/all_to_all | solution.py:75
  510.8 4.6 all-to-all-done.2
  515.4 2.3 gather_fusion
  (78 shorter events, 8.8 us)
Async XLA Ops:
  11.6 10.3 %all-to-all-start = ((s32[8,128,1]{1,2,0:T(1,128)}), s32[8,128,1]{1,2,0:T(1,128)S(1)}, u32[]{:S(2)}, u32[]{:S(2)}) async-start(s32[8,128,1]{1,2,0:T(1,128)} %bitcast.5), calls=%async_computation | async-start | bytes 8192 | tf_op jit(solution)/shard_map/all_to_all | solution.py:55
  21.9 25.4 %all-to-all-start.1 = ((bf16[8,128,768]{2,1,0:T(8,128)(2,1)}), bf16[8,128,768]{2,1,0:T(8,128)(2,1)S(1)}, u32[]{:S(2)}, u32[]{:S(2)}) async-start(bf16[8,128,768]{2,1,0:T(8,128)(2,1)} %bitcast.14), calls=%async_computation.1 | async-start | bytes 3145728 | tf_op jit(solution)/shard_map/all_to_all | solution.py:54
  26.6 158.5 %reduce-scatter.4.cloned.1.call-start = ((), (), s32[]{:S(2)}) async-start(), calls=%async_computation.4 | async-start | bytes 20471808
  47.3 13.3 %copy-start.21 = (bf16[8,128,768]{2,1,0:T(8,128)(2,1)}, bf16[8,128,768]{2,1,0:T(8,128)(2,1)S(1)}, u32[]{:S(2)}) copy-start(bf16[8,128,768]{2,1,0:T(8,128)(2,1)S(1)} %all-to-all-done.1) | copy-start | bytes 4718596
  185.1 268.3 %copy-start = (f32[392,768]{1,0:T(8,128)S(1)}, f32[392,768]{1,0:T(8,128)}, u32[]{:S(2)}) copy-start(f32[392,768]{1,0:T(8,128)} %reduce-scatter.4.cloned.1.call-done) | copy-start | bytes 3612676
  188.1 221.8 %copy-start.23 = (bf16[392,768]{1,0:T(8,128)(2,1)}, bf16[392,768]{1,0:T(8,128)(2,1)S(1)}, u32[]{:S(2)}) copy-start(bf16[392,768]{1,0:T(8,128)(2,1)S(1)} %multiply_convert_fusion) | copy-start | bytes 1806340
  188.1 17.8 %collective-permute-start = (bf16[392,768]{1,0:T(8,128)(2,1)S(1)}, bf16[392,768]{1,0:T(8,128)(2,1)S(1)}, u32[]{:S(2)}, u32[]{:S(2)}) collective-permute-start(bf16[392,768]{1,0:T(8,128)(2,1)S(1)} %multiply_convert_fusion), channel_id=1, source_target_pairs={{0,8},{8,16},{16,24},{24,32},{32,40},{40,48},{48,56},{56,64},{64,7... | collective-permute-start | bytes 1806344 | tf_op jit(solution)/shard_map/ppermute | solution.py:16
  205.9 16.8 %collective-permute-start.1 = (bf16[392,768]{1,0:T(8,128)(2,1)S(1)}, bf16[392,768]{1,0:T(8,128)(2,1)S(1)}, u32[]{:S(2)}, u32[]{:S(2)}) collective-permute-start(bf16[392,768]{1,0:T(8,128)(2,1)S(1)} %collective-permute-done), channel_id=1, source_target_pairs={{0,8},{8,16},{16,24},{24,32},{32,40},{40,48},{48,56},{56,64},{64,7... | collective-permute-start | bytes 1806344 | tf_op jit(solution)/shard_map/ppermute | solution.py:16
  222.7 15.9 %collective-permute-start.2 = (bf16[392,768]{1,0:T(8,128)(2,1)S(1)}, bf16[392,768]{1,0:T(8,128)(2,1)S(1)}, u32[]{:S(2)}, u32[]{:S(2)}) collective-permute-start(bf16[392,768]{1,0:T(8,128)(2,1)S(1)} %collective-permute-done.1), channel_id=1, source_target_pairs={{0,8},{8,16},{16,24},{24,32},{32,40},{40,48},{48,56},{56,64},{64,7... | collective-permute-start | bytes 1806344 | tf_op jit(solution)/shard_map/ppermute | solution.py:16
  238.6 14.9 %collective-permute-start.3 = (bf16[392,768]{1,0:T(8,128)(2,1)S(1)}, bf16[392,768]{1,0:T(8,128)(2,1)S(1)}, u32[]{:S(2)}, u32[]{:S(2)}) collective-permute-start(bf16[392,768]{1,0:T(8,128)(2,1)S(1)} %collective-permute-done.2), channel_id=1, source_target_pairs={{0,8},{8,16},{16,24},{24,32},{32,40},{40,48},{48,56},{56,64},{64,7... | collective-permute-start | bytes 1806344 | tf_op jit(solution)/shard_map/ppermute | solution.py:16
  253.5 0.8 copy-start.1
  254.3 14.0 %collective-permute-start.4 = (bf16[392,768]{1,0:T(8,128)(2,1)S(1)}, bf16[392,768]{1,0:T(8,128)(2,1)S(1)}, u32[]{:S(2)}, u32[]{:S(2)}) collective-permute-start(bf16[392,768]{1,0:T(8,128)(2,1)S(1)} %collective-permute-done.3), channel_id=1, source_target_pairs={{0,8},{8,16},{16,24},{24,32},{32,40},{40,48},{48,56},{56,64},{64,7... | collective-permute-start | bytes 1806344 | tf_op jit(solution)/shard_map/ppermute | solution.py:16
  268.4 0.8 copy-start.3
  269.2 13.1 %collective-permute-start.5 = (bf16[392,768]{1,0:T(8,128)(2,1)S(1)}, bf16[392,768]{1,0:T(8,128)(2,1)S(1)}, u32[]{:S(2)}, u32[]{:S(2)}) collective-permute-start(bf16[392,768]{1,0:T(8,128)(2,1)S(1)} %collective-permute-done.4), channel_id=1, source_target_pairs={{0,8},{8,16},{16,24},{24,32},{32,40},{40,48},{48,56},{56,64},{64,7... | collective-permute-start | bytes 1806344 | tf_op jit(solution)/shard_map/ppermute | solution.py:16
  282.3 0.8 copy-start.5
  283.1 12.2 %collective-permute-start.6 = (bf16[392,768]{1,0:T(8,128)(2,1)S(1)}, bf16[392,768]{1,0:T(8,128)(2,1)S(1)}, u32[]{:S(2)}, u32[]{:S(2)}) collective-permute-start(bf16[392,768]{1,0:T(8,128)(2,1)S(1)} %collective-permute-done.5), channel_id=1, source_target_pairs={{0,8},{8,16},{16,24},{24,32},{32,40},{40,48},{48,56},{56,64},{64,7... | collective-permute-start | bytes 1806344 | tf_op jit(solution)/shard_map/ppermute | solution.py:16
  295.3 0.8 copy-start.7
  296.1 12.3 %collective-permute-start.7 = (bf16[392,768]{1,0:T(8,128)(2,1)S(1)}, bf16[392,768]{1,0:T(8,128)(2,1)S(1)}, u32[]{:S(2)}, u32[]{:S(2)}) collective-permute-start(bf16[392,768]{1,0:T(8,128)(2,1)S(1)} %collective-permute-done.6), channel_id=1, source_target_pairs={{0,8},{8,16},{16,24},{24,32},{32,40},{40,48},{48,56},{56,64},{64,7... | collective-permute-start | bytes 1806344 | tf_op jit(solution)/shard_map/ppermute | solution.py:16
  308.4 0.9 copy-start.9
  309.3 13.4 %collective-permute-start.8 = (bf16[392,768]{1,0:T(8,128)(2,1)S(1)}, bf16[392,768]{1,0:T(8,128)(2,1)S(1)}, u32[]{:S(2)}, u32[]{:S(2)}) collective-permute-start(bf16[392,768]{1,0:T(8,128)(2,1)S(1)} %collective-permute-done.7), channel_id=1, source_target_pairs={{0,8},{8,16},{16,24},{24,32},{32,40},{40,48},{48,56},{56,64},{64,7... | collective-permute-start | bytes 1806344 | tf_op jit(solution)/shard_map/ppermute | solution.py:16
  322.7 0.9 copy-start.11
  323.6 14.4 %collective-permute-start.9 = (bf16[392,768]{1,0:T(8,128)(2,1)S(1)}, bf16[392,768]{1,0:T(8,128)(2,1)S(1)}, u32[]{:S(2)}, u32[]{:S(2)}) collective-permute-start(bf16[392,768]{1,0:T(8,128)(2,1)S(1)} %collective-permute-done.8), channel_id=1, source_target_pairs={{0,8},{8,16},{16,24},{24,32},{32,40},{40,48},{48,56},{56,64},{64,7... | collective-permute-start | bytes 1806344 | tf_op jit(solution)/shard_map/ppermute | solution.py:16
  338.0 0.8 copy-start.13
  338.8 15.6 %collective-permute-start.10 = (bf16[392,768]{1,0:T(8,128)(2,1)S(1)}, bf16[392,768]{1,0:T(8,128)(2,1)S(1)}, u32[]{:S(2)}, u32[]{:S(2)}) collective-permute-start(bf16[392,768]{1,0:T(8,128)(2,1)S(1)} %collective-permute-done.9), channel_id=1, source_target_pairs={{0,8},{8,16},{16,24},{24,32},{32,40},{40,48},{48,56},{56,64},{64,7... | collective-permute-start | bytes 1806344 | tf_op jit(solution)/shard_map/ppermute | solution.py:16
  354.3 0.8 copy-start.15
  355.1 16.6 %collective-permute-start.11 = (bf16[392,768]{1,0:T(8,128)(2,1)S(1)}, bf16[392,768]{1,0:T(8,128)(2,1)S(1)}, u32[]{:S(2)}, u32[]{:S(2)}) collective-permute-start(bf16[392,768]{1,0:T(8,128)(2,1)S(1)} %collective-permute-done.10), channel_id=1, source_target_pairs={{0,8},{8,16},{16,24},{24,32},{32,40},{40,48},{48,56},{56,64},{64,7... | collective-permute-start | bytes 1806344 | tf_op jit(solution)/shard_map/ppermute | solution.py:16
  371.8 0.8 copy-start.17
  372.6 17.7 %collective-permute-start.12 = (bf16[392,768]{1,0:T(8,128)(2,1)S(1)}, bf16[392,768]{1,0:T(8,128)(2,1)S(1)}, u32[]{:S(2)}, u32[]{:S(2)}) collective-permute-start(bf16[392,768]{1,0:T(8,128)(2,1)S(1)} %collective-permute-done.11), channel_id=1, source_target_pairs={{0,8},{8,16},{16,24},{24,32},{32,40},{40,48},{48,56},{56,64},{64,7... | collective-permute-start | bytes 1806344 | tf_op jit(solution)/shard_map/ppermute | solution.py:16
  390.3 0.8 copy-start.19
  391.1 18.7 %collective-permute-start.13 = (bf16[392,768]{1,0:T(8,128)(2,1)S(1)}, bf16[392,768]{1,0:T(8,128)(2,1)}, u32[]{:S(2)}, u32[]{:S(2)}) collective-permute-start(bf16[392,768]{1,0:T(8,128)(2,1)S(1)} %collective-permute-done.12), channel_id=1, source_target_pairs={{0,8},{8,16},{16,24},{24,32},{32,40},{40,48},{48,56},{56,64},{64,7... | collective-permute-start | bytes 1806344 | tf_op jit(solution)/shard_map/ppermute | solution.py:16
  409.9 17.5 %collective-permute-start.14 = (bf16[392,768]{1,0:T(8,128)(2,1)}, bf16[392,768]{1,0:T(8,128)(2,1)}, u32[]{:S(2)}, u32[]{:S(2)}) collective-permute-start(bf16[392,768]{1,0:T(8,128)(2,1)} %collective-permute-done.13), channel_id=1, source_target_pairs={{0,8},{8,16},{16,24},{24,32},{32,40},{40,48},{48,56},{56,64},{64,7... | collective-permute-start | bytes 1806344 | tf_op jit(solution)/shard_map/ppermute | solution.py:16
  409.9 48.3 %copy-start.20 = (bf16[392,768]{1,0:T(8,128)(2,1)S(1)}, bf16[392,768]{1,0:T(8,128)(2,1)}, u32[]{:S(2)}) copy-start(bf16[392,768]{1,0:T(8,128)(2,1)} %copy-done.19) | copy-start | bytes 1806340
  409.9 49.2 %copy-start.18 = (bf16[392,768]{1,0:T(8,128)(2,1)S(1)}, bf16[392,768]{1,0:T(8,128)(2,1)}, u32[]{:S(2)}) copy-start(bf16[392,768]{1,0:T(8,128)(2,1)} %copy-done.17) | copy-start | bytes 1806340
  409.9 50.0 %copy-start.16 = (bf16[392,768]{1,0:T(8,128)(2,1)S(1)}, bf16[392,768]{1,0:T(8,128)(2,1)}, u32[]{:S(2)}) copy-start(bf16[392,768]{1,0:T(8,128)(2,1)} %copy-done.15) | copy-start | bytes 1806340
  409.9 50.9 %copy-start.14 = (bf16[392,768]{1,0:T(8,128)(2,1)S(1)}, bf16[392,768]{1,0:T(8,128)(2,1)}, u32[]{:S(2)}) copy-start(bf16[392,768]{1,0:T(8,128)(2,1)} %copy-done.13) | copy-start | bytes 1806340
  409.9 51.8 %copy-start.12 = (bf16[392,768]{1,0:T(8,128)(2,1)S(1)}, bf16[392,768]{1,0:T(8,128)(2,1)}, u32[]{:S(2)}) copy-start(bf16[392,768]{1,0:T(8,128)(2,1)} %copy-done.11) | copy-start | bytes 1806340
  409.9 52.7 %copy-start.10 = (bf16[392,768]{1,0:T(8,128)(2,1)S(1)}, bf16[392,768]{1,0:T(8,128)(2,1)}, u32[]{:S(2)}) copy-start(bf16[392,768]{1,0:T(8,128)(2,1)} %copy-done.9) | copy-start | bytes 1806340
  409.9 53.5 %copy-start.8 = (bf16[392,768]{1,0:T(8,128)(2,1)S(1)}, bf16[392,768]{1,0:T(8,128)(2,1)}, u32[]{:S(2)}) copy-start(bf16[392,768]{1,0:T(8,128)(2,1)} %copy-done.7) | copy-start | bytes 1806340
  409.9 54.4 %copy-start.6 = (bf16[392,768]{1,0:T(8,128)(2,1)S(1)}, bf16[392,768]{1,0:T(8,128)(2,1)}, u32[]{:S(2)}) copy-start(bf16[392,768]{1,0:T(8,128)(2,1)} %copy-done.5) | copy-start | bytes 1806340
  409.9 55.3 %copy-start.4 = (bf16[392,768]{1,0:T(8,128)(2,1)S(1)}, bf16[392,768]{1,0:T(8,128)(2,1)}, u32[]{:S(2)}) copy-start(bf16[392,768]{1,0:T(8,128)(2,1)} %copy-done.3) | copy-start | bytes 1806340
  409.9 56.1 %copy-start.2 = (bf16[392,768]{1,0:T(8,128)(2,1)S(1)}, bf16[392,768]{1,0:T(8,128)(2,1)}, u32[]{:S(2)}) copy-start(bf16[392,768]{1,0:T(8,128)(2,1)} %copy-done.1) | copy-start | bytes 1806340
  429.3 41.3 %copy-start.22 = (bf16[8,128,768]{2,1,0:T(8,128)(2,1)S(1)}, bf16[8,128,768]{2,1,0:T(8,128)(2,1)}, u32[]{:S(2)}) copy-start(bf16[8,128,768]{2,1,0:T(8,128)(2,1)} %copy-done.21) | copy-start | bytes 4718596
  490.2 25.2 %all-to-all-start.2 = ((f32[8,128,1]{1,2,0:T(1,128)}), f32[8,128,1]{1,2,0:T(1,128)S(1)}, u32[]{:S(2)}, u32[]{:S(2)}) async-start(f32[8,128,1]{1,2,0:T(1,128)} %bitcast.17), calls=%async_computation.2 | async-start | bytes 8192 | tf_op jit(solution)/shard_map/all_to_all | solution.py:75
Sparse Core Ops, SparseCore 0:
  60.8 124.3 reduce-scatter.3
